TPU v7x, 512 devices: a whole 4x4x16 slice. The times are simulated.
512 devices in a mesh: dp: 16 (over y, x), seq: 32 (over z, core).
Axes of the slice: x: 4, y: 4, z: 16, core: 2. Of those that a mesh axis runs over, the one named last changes fastest.
Arguments:
- hidden: bfloat16 [16, 4096, 1280], P('dp', 'seq'), may hold values from -6 to 6
- gate_probs: float32 [16, 2, 4096], P('dp', None, 'seq'), may hold values from 0.05 to 0.95
- expert_ids: int32 [16, 2, 4096], P('dp', None, 'seq'), may hold values from 0 to 31, as said below
- slot_ids: int32 [16, 2, 4096], P('dp', None, 'seq'), may hold values from 0 to 2, as said below
- mask_pos: int32 [16, 2048], P('dp', 'seq'), may hold values from 0 to 127, as said below
- distractors: int32 [16, 10, 2048], P('dp', None, 'seq'), may hold values from 0 to 2047, as said below
- targets: bfloat16 [16, 2048, 1280], P('dp', 'seq'), may hold values from -6 to 6
- weight_in: bfloat16 [32, 1280, 5120], P('seq', None, 'dp'), may hold values from -0.15625 to 0.15625
- weight_out: bfloat16 [32, 5120, 1280], P('seq', 'dp'), may hold values from -0.078125 to 0.078125
Outputs:
- frame_loss: float32 [16, 2048], P('dp', 'seq')
- gate_grad: float32 [16, 2, 4096], P('dp', None, 'seq')
- grad_hidden: bfloat16 [16, 4096, 1280], P('dp', 'seq')
- grad_weight_in: bfloat16 [32, 1280, 5120], P('seq', None, 'dp')
- grad_weight_out: bfloat16 [32, 5120, 1280], P('seq', 'dp')
Inputs may be any that keep to these rules, and one draw needn't show every extreme that they name: expert_ids[r, 0, f] and expert_ids[r, 1, f] differ. In each device's block of 128 frames every expert is the first choice of exactly 4 frames. slot_ids[r, k, f] is the number of assignments to the same expert that come earlier in the same block of 128 frames (frames in order, the first choice before the second), replaced by 2 when it reaches 2; 2 marks a dropped assignment. Each of the 2 slots of every expert is taken by exactly one assignment of every block. `mask_pos`: each device's 64 entries are distinct and rising. `distractors`: entry [r, j, i] indexes the masked frames of recording r and differs from i. Of the 640 entries of one device's masked frames, exactly 20 lie in each block of 64 masked frames.
All inputs are finite; a program needn't handle non-finite values.
Results may differ from a plain program's by a relative error of at most 0.008.
Values may be sent and summed in bfloat16 or wider, within the bound.
A program may use at most 64 MiB of HBM per device.

v0:
```python
import jax
import jax.numpy as jnp
from jax import lax
from jax.sharding import PartitionSpec as P

CAP = 2


sharpness_divisor = 0.1
objective_scaling = 64.0
norm_eps = 1e-06


def gelu_slope(preact):
    return jax.vjp(jax.nn.gelu, preact)[1](jnp.ones_like(preact))[0]


def slot_tables(expert_picks, slot_picks, gate_values, experts_all):
    kept_mask = slot_picks < CAP
    slot_width = experts_all * CAP
    slot_index = jnp.where(kept_mask, expert_picks * CAP + slot_picks, slot_width)
    matches = slot_index[:, :, None] == jnp.arange(slot_width, dtype=jnp.int32)[None, None, :]
    frame_count = expert_picks.shape[1]
    frame_iota = jnp.arange(frame_count, dtype=jnp.int32)
    slot_frame = jnp.sum(jnp.where(matches, frame_iota[None, :, None], 0), axis=(0, 1))
    slot_gate = jnp.sum(jnp.where(matches, gate_values[:, :, None], 0.0), axis=(0, 1))
    return (kept_mask, jnp.minimum(slot_index, slot_width - 1), slot_frame, slot_gate)


def contrast_loss(context, own_targets, fetched):
    context_norm = jnp.sqrt(jnp.sum(context * context, axis=-1) + norm_eps)
    context_unit = context / context_norm[:, None]
    candidates = jnp.concatenate([own_targets[None], fetched], axis=0).astype(jnp.float32)
    target_norm = jnp.sqrt(jnp.sum(candidates * candidates, axis=-1) + norm_eps)
    target_unit = candidates / target_norm[..., None]
    angular_agreement = jnp.sum(context_unit[None] * target_unit, axis=-1)
    raw_match_values = angular_agreement / sharpness_divisor
    log_total = jnp.log(jnp.sum(jnp.exp(raw_match_values), axis=0))
    frame_loss = log_total - raw_match_values[0]
    normalized_exponential_share = jnp.exp(raw_match_values - log_total[None])
    correct_match_value = (jnp.arange(raw_match_values.shape[0]) == 0).astype(jnp.float32)[:, None]
    raw_match_derivative_scaling = (
        objective_scaling * (normalized_exponential_share - correct_match_value) / sharpness_divisor
    )
    grad_unit = jnp.sum(raw_match_derivative_scaling[..., None] * target_unit, axis=0)
    along = jnp.sum(grad_unit * context_unit, axis=-1)
    grad_context = (grad_unit - along[:, None] * context_unit) / context_norm[:, None]
    return (frame_loss, grad_context)


def dispatch_rows(outgoing):
    owned = lax.all_to_all(outgoing, "seq", split_axis=0, concat_axis=0, tiled=True)
    return lax.all_gather(owned, "dp", axis=0, tiled=True)


def collect_rows(partial_rows, model_width):
    groups = lax.axis_size("dp")
    pieces = lax.all_to_all(
        partial_rows.astype(jnp.bfloat16), "dp", split_axis=0, concat_axis=0, tiled=True
    )
    summed = jnp.sum(pieces.reshape(groups, -1, model_width).astype(jnp.float32), axis=0)
    return lax.all_to_all(
        summed.astype(jnp.bfloat16), "seq", split_axis=0, concat_axis=0, tiled=True
    )


def local(
    hidden, gate_probs, expert_ids, slot_ids, mask_pos, distractors, targets, weight_in, weight_out
):
    frame_rows = hidden[0]
    model_width = frame_rows.shape[1]
    local_experts = weight_in.shape[0]
    experts_all = local_experts * lax.axis_size("seq")
    gate_values = gate_probs[0]
    kept_mask, slot_index, slot_frame, slot_gate = slot_tables(
        expert_ids[0], slot_ids[0], gate_values, experts_all
    )
    outgoing = jnp.take(frame_rows, slot_frame, axis=0)
    gathered = dispatch_rows(outgoing)
    grouped = gathered.reshape(-1, local_experts, CAP, model_width)
    preact = jnp.einsum("aecd,edh->aech", grouped, weight_in, preferred_element_type=jnp.float32)
    activation = jax.nn.gelu(preact).astype(jnp.bfloat16)
    partial_rows = jnp.einsum(
        "aech,ehd->aecd", activation, weight_out, preferred_element_type=jnp.float32
    )
    returned = collect_rows(partial_rows.reshape(-1, model_width), model_width)
    picked = jnp.take(returned, slot_index.reshape(-1), axis=0)
    picked = picked.reshape(slot_index.shape + (model_width,)).astype(jnp.float32)
    weight = jnp.where(kept_mask, gate_values, 0.0)
    mixed_rows = (
        frame_rows.astype(jnp.float32) + jnp.sum(weight[:, :, None] * picked, axis=0)
    ).astype(jnp.bfloat16)
    context = jnp.take(mixed_rows, mask_pos[0], axis=0).astype(jnp.float32)
    own_targets = targets[0]
    everyone = lax.all_gather(own_targets, "seq", axis=0, tiled=True)
    fetched = jnp.take(everyone, distractors[0].reshape(-1), axis=0)
    fetched = fetched.reshape(distractors.shape[1], distractors.shape[2], model_width)
    frame_loss, grad_context = contrast_loss(context, own_targets, fetched)
    grad_mixed = jnp.zeros(frame_rows.shape, jnp.float32).at[mask_pos[0]].set(grad_context)
    gate_grad = jnp.where(kept_mask, jnp.sum(grad_mixed[None] * picked, axis=-1), 0.0)
    grad_out = (jnp.take(grad_mixed, slot_frame, axis=0) * slot_gate[:, None]).astype(jnp.bfloat16)
    grad_rows = dispatch_rows(grad_out).reshape(grouped.shape)
    grad_act = jnp.einsum(
        "aecd,ehd->aech", grad_rows, weight_out, preferred_element_type=jnp.float32
    )
    grad_pre = (grad_act * gelu_slope(preact)).astype(jnp.bfloat16)
    grad_weight_out = jnp.einsum(
        "aech,aecd->ehd", activation, grad_rows, preferred_element_type=jnp.float32
    ).astype(jnp.bfloat16)
    grad_weight_in = jnp.einsum(
        "aecd,aech->edh", grouped, grad_pre, preferred_element_type=jnp.float32
    ).astype(jnp.bfloat16)
    grad_partial = jnp.einsum(
        "aech,edh->aecd", grad_pre, weight_in, preferred_element_type=jnp.float32
    )
    grad_back = collect_rows(grad_partial.reshape(-1, model_width), model_width)
    grad_inputs = jnp.take(grad_back, slot_index.reshape(-1), axis=0)
    grad_inputs = grad_inputs.reshape(slot_index.shape + (model_width,)).astype(jnp.float32)
    added = jnp.sum(jnp.where(kept_mask[:, :, None], grad_inputs, 0.0), axis=0)
    grad_hidden = (grad_mixed + added).astype(jnp.bfloat16)
    return (frame_loss[None], gate_grad[None], grad_hidden[None], grad_weight_in, grad_weight_out)


def solution(mesh):
    return jax.shard_map(
        local,
        mesh=mesh,
        in_specs=(
            P("dp", "seq", None),
            P("dp", None, "seq"),
            P("dp", None, "seq"),
            P("dp", None, "seq"),
            P("dp", "seq"),
            P("dp", None, "seq"),
            P("dp", "seq", None),
            P("seq", None, "dp"),
            P("seq", "dp", None),
        ),
        out_specs=(
            P("dp", "seq"),
            P("dp", None, "seq"),
            P("dp", "seq", None),
            P("seq", None, "dp"),
            P("seq", "dp", None),
        ),
        check_vma=False,
    )
```

profile of v0, /device:TPU:1, one launch (start us, length us, event | category | flops | bytes accessed | tf_op | source)
XLA Modules:
  0.0 386.1 jit_solution(10807900189072410357)
XLA Ops:
  7.2 0.8 bitcast_select_fusion.1
  8.1 1.9 gather_fusion.2
  10.2 33.7 %all_to_all.57 = bf16[32,2,1280]{2,1,0:T(2,128)(2,1)S(1)} all-to-all(bf16[32,2,1280]{2,1,0:T(2,128)(2,1)S(1)} %all_to_all.38), channel_id=1, replica_groups=mesh['dp'=16,'seq'=32] {'seq'}, dimensions={0} | all-to-all | bytes 327680 | tf_op jit(solution)/shard_map/all_to_all | solution.py:52
  43.9 0.7 all_to_all.40
  44.7 0.7 all-gather.9.cloned.1.call-update
  45.4 52.9 %all-gather.5.cloned.1.call-done = bf16[1024,1280]{1,0:T(8,128)(2,1)} async-done(((bf16[64,1280]{1,0:T(8,128)(2,1)}), bf16[1024,1280]{1,0:T(8,128)(2,1)}) %all-gather.5.cloned.1.call-update) | async-done | bytes 2621456 | tf_op jit(solution)/shard_map/all_gather | solution.py:53
  98.3 5.3 %reshape.294 = bf16[512,2,1280]{2,1,0:T(2,128)(2,1)S(1)} reshape(bf16[1024,1280]{1,0:T(8,128)(2,1)} %all-gather.5.cloned.1.call-done) | data formatting | bytes 5242880 | tf_op jit(solution)/shard_map/reshape.3
  103.6 2.8 fusion.13
  106.4 1.7 fusion.1
  108.1 2.7 copy.21
  110.8 2.5 convert_element_type.101
  113.3 4.2 %all-to-all-start.1 = ((bf16[16,64,1280]{2,1,0:T(8,128)(2,1)}), bf16[16,64,1280]{2,1,0:T(8,128)(2,1)S(1)}, u32[]{:S(2)}, u32[]{:S(2)}) async-start(bf16[16,64,1280]{2,1,0:T(8,128)(2,1)} %convert_element_type.101), calls=%async_computation.1 | async-start | bytes 5242880 | tf_op jit(solution)/shard_map/all_to_all | solution.py:58
  118.2 35.1 %all-to-all-done.1 = bf16[16,64,1280]{2,1,0:T(8,128)(2,1)S(1)} async-done(((bf16[16,64,1280]{2,1,0:T(8,128)(2,1)}), bf16[16,64,1280]{2,1,0:T(8,128)(2,1)S(1)}, u32[]{:S(2)}, u32[]{:S(2)}) %all-to-all-start.1) | async-done | bytes 2621472 | tf_op jit(solution)/shard_map/all_to_all | solution.py:58
  153.2 1.1 reduce_sum.130
  154.3 1.6 all_to_all.42
  155.9 15.4 %all-to-all-start.2 = ((bf16[32,2,1280]{2,1,0:T(2,128)(2,1)}), bf16[32,2,1280]{2,1,0:T(2,128)(2,1)S(1)}, u32[]{:S(2)}, u32[]{:S(2)}) async-start(bf16[32,2,1280]{2,1,0:T(2,128)(2,1)} %all_to_all.42), calls=%async_computation.2 | async-start | bytes 327680 | tf_op jit(solution)/shard_map/all_to_all | solution.py:62
  171.6 16.9 %all-to-all-done.2 = bf16[32,2,1280]{2,1,0:T(2,128)(2,1)S(1)} async-done(((bf16[32,2,1280]{2,1,0:T(2,128)(2,1)}), bf16[32,2,1280]{2,1,0:T(2,128)(2,1)S(1)}, u32[]{:S(2)}, u32[]{:S(2)}) %all-to-all-start.2) | async-done | bytes 163872 | tf_op jit(solution)/shard_map/all_to_all | solution.py:62
  188.6 1.3 gather_fusion.3
  190.1 0.8 copy-done.1
  191.0 0.7 gather_fusion.4
  192.0 0.8 convert_divide_fusion.1
  192.8 7.7 %gather_fusion = bf16[640,1280]{1,0:T(8,128)(2,1)S(1)} fusion(bf16[2048,1280]{1,0:T(8,128)(2,1)} %bitcast.116, s32[1024]{0:T(1024)S(1)} %pad_clamp_fusion.1), kind=kCustom, calls=%fused_computation.4 | custom fusion | bytes 3279360 | tf_op jit(solution)/shard_map/jit(_take)/gather | solution.py:96
  200.8 0.7 copy-done.2
  201.9 0.5 copy-done.5
  202.4 0.6 multiply_reduce_fusion.1
  203.2 0.6 multiply_reduce_fusion
  204.0 1.1 scatter_custom_fusion
  205.1 0.7 gather_fusion.1
  206.3 21.6 %all_to_all.58 = bf16[32,2,1280]{2,1,0:T(2,128)(2,1)S(1)} all-to-all(bf16[32,2,1280]{2,1,0:T(2,128)(2,1)S(1)} %multiply_convert_fusion.1), channel_id=1, replica_groups=mesh['dp'=16,'seq'=32] {'seq'}, dimensions={0} | all-to-all | bytes 327680 | tf_op jit(solution)/shard_map/all_to_all | solution.py:52
  227.9 0.7 all_to_all.46
  228.6 49.6 %all-gather.7.cloned.1.call-done = bf16[1024,1280]{1,0:T(8,128)(2,1)} async-done(((bf16[64,1280]{1,0:T(8,128)(2,1)}), bf16[1024,1280]{1,0:T(8,128)(2,1)}) %all-gather.7.cloned.1.call-update) | async-done | bytes 2621456 | tf_op jit(solution)/shard_map/all_gather | solution.py:53
  278.2 6.5 %reshape.298 = bf16[512,2,1280]{2,1,0:T(2,128)(2,1)} reshape(bf16[1024,1280]{1,0:T(8,128)(2,1)} %all-gather.7.cloned.1.call-done) | data formatting | bytes 5242880 | tf_op jit(solution)/shard_map/reshape.22
  284.7 3.8 fusion.33
  288.5 1.6 fusion.2
  290.1 4.3 %copy.23 = bf16[512,1,2,1280]{3,2,0,1:T(2,128)(2,1)} copy(bf16[512,1,2,1280]{3,0,2,1:T(8,128)(2,1)S(1)} %fusion.2) | data formatting | bytes 5242880 | tf_op jit(solution)/shard_map/convert_element_type | solution.py:59
  294.4 6.7 %convert_element_type.115 = bf16[16,64,1280]{2,1,0:T(8,128)(2,1)} reshape(bf16[512,1,2,1280]{3,2,0,1:T(2,128)(2,1)} %copy.23) | data formatting | bytes 5242880 | tf_op jit(solution)/shard_map/convert_element_type | solution.py:59
  301.1 4.4 %all-to-all-start.4 = ((bf16[16,64,1280]{2,1,0:T(8,128)(2,1)}), bf16[16,64,1280]{2,1,0:T(8,128)(2,1)}, u32[]{:S(2)}, u32[]{:S(2)}) async-start(bf16[16,64,1280]{2,1,0:T(8,128)(2,1)} %convert_element_type.115), calls=%async_computation.4 | async-start | bytes 5242880 | tf_op jit(solution)/shard_map/all_to_all | solution.py:58
  305.8 0.6 bitcast_select_fusion
  306.4 0.5 slice_subtract_fusion
  306.9 35.2 %all-to-all-done.4 = bf16[16,64,1280]{2,1,0:T(8,128)(2,1)} async-done(((bf16[16,64,1280]{2,1,0:T(8,128)(2,1)}), bf16[16,64,1280]{2,1,0:T(8,128)(2,1)}, u32[]{:S(2)}, u32[]{:S(2)}) %all-to-all-start.4) | async-done | bytes 2621472 | tf_op jit(solution)/shard_map/all_to_all | solution.py:58
  342.1 2.1 reduce_sum.143
  344.2 0.7 all_to_all.48
  344.9 15.1 %all-to-all-start.5 = ((bf16[32,2,1280]{2,1,0:T(2,128)(2,1)}), bf16[32,2,1280]{2,1,0:T(2,128)(2,1)S(1)}, u32[]{:S(2)}, u32[]{:S(2)}) async-start(bf16[32,2,1280]{2,1,0:T(2,128)(2,1)} %all_to_all.48), calls=%async_computation.5 | async-start | bytes 327680 | tf_op jit(solution)/shard_map/all_to_all | solution.py:62
  360.1 3.8 fusion.5
  363.9 2.2 fusion.6
  366.1 11.1 %all-to-all-done.5 = bf16[32,2,1280]{2,1,0:T(2,128)(2,1)S(1)} async-done(((bf16[32,2,1280]{2,1,0:T(2,128)(2,1)}), bf16[32,2,1280]{2,1,0:T(2,128)(2,1)S(1)}, u32[]{:S(2)}, u32[]{:S(2)}) %all-to-all-start.5) | async-done | bytes 163872 | tf_op jit(solution)/shard_map/all_to_all | solution.py:62
  377.2 1.3 gather_fusion.5
  378.8 0.8 fusion.43
  (80 shorter events, 3.9 us)
Async XLA Ops:
  7.2 99.2 %copy-start = (bf16[1,320,1280]{2,1,0:T(8,128)(2,1)S(1)}, bf16[1,320,1280]{2,1,0:T(8,128)(2,1)}, u32[]{:S(2)}) copy-start(bf16[1,320,1280]{2,1,0:T(8,128)(2,1)} %param.21) | copy-start | bytes 2457604
  7.2 91.1 %all-gather.5.cloned.1.call-start = ((), (), s32[]{:S(2)}) async-start(), calls=%async_computation.6 | async-start | bytes 2785280 | tf_op jit(solution)/shard_map/all_gather | solution.py:53
  44.6 148.2 %all-gather.9.cloned.1.call-start = ((), (), s32[]{:S(2)}) async-start(), calls=%async_computation.8 | async-start | bytes 5406720 | tf_op jit(solution)/shard_map/all_gather | solution.py:95
  103.6 2.8 copy-start.3
  106.4 1.7 copy-start.14
  113.3 4.3 %copy-start.6 = (s32[1,10,64]{2,0,1:T(1,128)S(1)}, s32[1,10,64]{2,0,1:T(1,128)}, u32[]{:S(2)}) copy-start(s32[1,10,64]{2,0,1:T(1,128)} %param.18) | copy-start | bytes 7684
  113.3 4.4 %copy-start.9 = (f32[1,2,128]{2,1,0:T(2,128)S(1)}, f32[1,2,128]{2,1,0:T(2,128)}, u32[]{:S(2)}) copy-start(f32[1,2,128]{2,1,0:T(2,128)} %param.14) | copy-start | bytes 3076
  113.3 4.7 %copy-start.7 = (s32[1,2,128]{2,1,0:T(2,128)S(1)}, s32[1,2,128]{2,1,0:T(2,128)}, u32[]{:S(2)}) copy-start(s32[1,2,128]{2,1,0:T(2,128)} %param.16) | copy-start | bytes 3076
  113.3 4.7 %copy-start.8 = (s32[1,2,128]{2,1,0:T(2,128)S(1)}, s32[1,2,128]{2,1,0:T(2,128)}, u32[]{:S(2)}) copy-start(s32[1,2,128]{2,1,0:T(2,128)} %param.15) | copy-start | bytes 3076
  113.3 4.7 %copy-start.11 = (s32[1,64]{1,0:T(1,128)S(1)}, s32[1,64]{1,0:T(1,128)}, u32[]{:S(2)}) copy-start(s32[1,64]{1,0:T(1,128)} %param.17) | copy-start | bytes 772
  113.3 39.9 %all-to-all-start.1 = ((bf16[16,64,1280]{2,1,0:T(8,128)(2,1)}), bf16[16,64,1280]{2,1,0:T(8,128)(2,1)S(1)}, u32[]{:S(2)}, u32[]{:S(2)}) async-start(bf16[16,64,1280]{2,1,0:T(8,128)(2,1)} %convert_element_type.101), calls=%async_computation.1 | async-start | bytes 5242880 | tf_op jit(solution)/shard_map/all_to_all | solution.py:58
  155.9 32.6 %all-to-all-start.2 = ((bf16[32,2,1280]{2,1,0:T(2,128)(2,1)}), bf16[32,2,1280]{2,1,0:T(2,128)(2,1)S(1)}, u32[]{:S(2)}, u32[]{:S(2)}) async-start(bf16[32,2,1280]{2,1,0:T(2,128)(2,1)} %all_to_all.42), calls=%async_computation.2 | async-start | bytes 327680 | tf_op jit(solution)/shard_map/all_to_all | solution.py:62
  171.3 106.9 %all-gather.7.cloned.1.call-start = ((), (), s32[]{:S(2)}) async-start(), calls=%async_computation.7 | async-start | bytes 2785280 | tf_op jit(solution)/shard_map/all_gather | solution.py:53
  190.0 1.0 copy-start.1
  200.5 0.9 copy-start.2
  201.4 1.0 copy-start.5
  284.7 3.8 copy-start.10
  288.5 1.6 copy-start.12
  301.1 41.0 %all-to-all-start.4 = ((bf16[16,64,1280]{2,1,0:T(8,128)(2,1)}), bf16[16,64,1280]{2,1,0:T(8,128)(2,1)}, u32[]{:S(2)}, u32[]{:S(2)}) async-start(bf16[16,64,1280]{2,1,0:T(8,128)(2,1)} %convert_element_type.115), calls=%async_computation.4 | async-start | bytes 5242880 | tf_op jit(solution)/shard_map/all_to_all | solution.py:58
  306.9 53.1 %copy-start.13 = (bf16[512,2,320]{0,2,1:T(8,128)(2,1)S(1)}, bf16[512,2,320]{0,2,1:T(8,128)(2,1)}, u32[]{:S(2)}) copy-start(bf16[512,2,320]{0,2,1:T(8,128)(2,1)} %copy-done.12) | copy-start | bytes 1966084
  344.9 32.2 %all-to-all-start.5 = ((bf16[32,2,1280]{2,1,0:T(2,128)(2,1)}), bf16[32,2,1280]{2,1,0:T(2,128)(2,1)S(1)}, u32[]{:S(2)}, u32[]{:S(2)}) async-start(bf16[32,2,1280]{2,1,0:T(2,128)(2,1)} %all_to_all.48), calls=%async_computation.5 | async-start | bytes 327680 | tf_op jit(solution)/shard_map/all_to_all | solution.py:62
  360.1 3.8 copy-start.4
  360.1 3.8 copy-start.15
Sparse Core Ops, SparseCore 0:
  44.8 53.4 all-gather.4
  100.4 76.2 all-gather.8
  228.8 49.4 all-gather.6
where the time goes:
time: 387 us; the launch traced here: 386 us
  waiting for transfers between devices  201 us (52%)
  blocking collectives  55.3 us (14%)
  local copies, waits for them, and re-layouts  48 us (12%)
  starting transfers between devices  39.4 us (10%)
  matrix products  15.8 us (4%)
  between operations  14.3 us (4%)
  other arithmetic  11.9 us (3%)
    all_gather x2, waiting for transfers between devices, dispatch_rows(): return lax.all_gather(owned, 'dp', axis=0, tiled=True)  102 us
    all_to_all x2, waiting for transfers between devices, collect_rows(): lax.all_to_all(partial_rows.astype(jnp.bfloat16), 'dp', split_axis=0, con...  70.2 us
    all_to_all x2, blocking collectives, dispatch_rows(): lax.all_to_all(outgoing, 'seq', split_axis=0, concat_axis=0, tiled=True)  55.3 us
    all_to_all x2, starting transfers between devices, collect_rows(): lax.all_to_all(summed.astype(jnp.bfloat16), 'seq', split_axis=0, concat_a...  30.5 us
    all_to_all x2, waiting for transfers between devices, collect_rows(): lax.all_to_all(summed.astype(jnp.bfloat16), 'seq', split_axis=0, concat_a...  28 us
    convert_element_type x4, local copies, waits for them, and re-layouts, collect_rows(): partial_rows.astype(jnp.bfloat16)  16.2 us
    another operation x2, local copies, waits for them, and re-layouts  11.7 us
    all_to_all x2, starting transfers between devices, collect_rows(): lax.all_to_all(partial_rows.astype(jnp.bfloat16), 'dp', split_axis=0, con...  8.65 us
  transfers between devices with their start and end apart: 7, of which 6 were waited for; matrix products, arithmetic and copies ran while one was open for 7% of the time, Pallas kernels for 0%

commit v1 on v0

v1 whole, which is shorter than its diff:
```python
import jax
import jax.numpy as jnp
from jax import lax
from jax.experimental import pallas as pl
from jax.experimental.pallas import tpu as pltpu
from jax.sharding import PartitionSpec as P

MESH = pl.DeviceIdType.MESH
BF = jnp.bfloat16
F32 = jnp.float32
NZ = 16
NS = 32
CHUNKS = 4
D = 1280
HID = 320
ROWS = 64
FR = 128
MK = 64
NEG = 10
EPS = 1e-06
SHARP = 0.1
SCALE = 64.0
DZ = [0] + [(h + 1) // 2 if h % 2 else NZ - h // 2 for h in range(1, NZ)]


def dot(a, b):
    return jnp.dot(a, b, preferred_element_type=F32)


def dot_nt(a, b):
    return lax.dot_general(a, b, (((1,), (1,)), ((), ())), preferred_element_type=F32)


def pieces(v):
    hi = v.astype(BF)
    lo = (v - hi.astype(F32)).astype(BF)
    return hi, lo


def gelu_parts(x):
    k = 0.7978845608028654
    x2 = x * x
    t = jnp.tanh(k * (x + 0.044715 * (x2 * x)))
    half = 0.5 * (1.0 + t)
    slope = half + 0.5 * x * (1.0 - t * t) * (k * (1.0 + (3 * 0.044715) * x2))
    return x * half, slope


def kernel(
    hid_ref, gate_ref, exp_ref, slot_ref, pos_ref, dis_ref, tgt_ref, win_ref, wout_ref,
    loss_ref, gg_ref, gh_ref, dwi_ref, dwo_ref,
    hid, gate, exps, slots, pos, dis, win, wout, wint, woutt,
    tgt, out, inn, grp, part, rsb, acc, rsa, rout, ret,
    act_t, grp_t, slope, gpre, lossv, ggv, ghv, dwiv, dwov,
    lsem, osem,
    ds, dr, gas, gar, gbs, gbr, bs, br, as_, ar, ts, tr,
    rgs, rgr, sbs, sbr,
):
    dp, s = lax.axis_index("dp"), lax.axis_index("seq")
    z, c = s // 2, s % 2
    y, x = dp // 4, dp % 4
    a = x + c * (y - x)
    b = y + c * (x - y)

    def dpi(aa, bb):
        return aa * (1 + 3 * c) + bb * (4 - 3 * c)

    apeer = {d: (dpi((a + d) % 4, b), s) for d in (1, 2, 3)}
    bpeer = {d: (dpi(a, (b + d) % 4), s) for d in (1, 2, 3)}

    def zpeer(k):
        return (dp, ((z + NZ - DZ[k // 2]) % NZ) * 2 + (c + k % 2) % 2)

    def zback(k):
        return (dp, ((z + DZ[k // 2]) % NZ) * 2 + (c + k % 2) % 2)

    zup = (dp, ((z + 1) % NZ) * 2 + c)
    zdn = (dp, ((z + NZ - 1) % NZ) * 2 + c)
    sib = (dp, z * 2 + 1 - c)

    def rc(src, dst, ssem, rsem, dev):
        return pltpu.make_async_remote_copy(
            src_ref=src, dst_ref=dst, send_sem=ssem, recv_sem=rsem, device_id=dev, device_id_type=MESH
        )

    barrier = pltpu.get_barrier_semaphore()
    for k in range(1, NS):
        pl.semaphore_signal(barrier, inc=1, device_id=zpeer(k), device_id_type=MESH)
    for d in (1, 2, 3):
        pl.semaphore_signal(barrier, inc=1, device_id=apeer[d], device_id_type=MESH)
        pl.semaphore_signal(barrier, inc=1, device_id=bpeer[d], device_id_type=MESH)

    loads = [
        (hid_ref, hid), (gate_ref, gate), (exp_ref, exps), (slot_ref, slots), (pos_ref, pos),
        (dis_ref, dis), (win_ref, win), (wout_ref, wout),
    ]
    loads = [pltpu.make_async_copy(p, q, lsem.at[i]) for i, (p, q) in enumerate(loads)]
    tloads = [
        pltpu.make_async_copy(tgt_ref.at[pl.ds(32 * h, 32)], tgt.at[z, c, h], lsem.at[len(loads) + h])
        for h in (0, 1)
    ]
    for cp in loads + tloads:
        cp.start()
    for cp in loads[:5]:
        cp.wait()

    row = lax.broadcasted_iota(jnp.int32, (ROWS, FR), 0)
    kk = row >> 1
    hh = kk >> 1
    dz = jnp.where((hh & 1) == 1, (hh + 1) >> 1, (NZ - (hh >> 1)) & (NZ - 1))
    want = (((z + NZ - dz) & (NZ - 1)) << 1) + ((c + (kk & 1)) & 1)
    cap = row & 1
    own_row = [
        jnp.where((exps[t : t + 1, :] == want) & (slots[t : t + 1, :] == cap), 1.0, 0.0) for t in (0, 1)
    ]
    gate_row = jnp.sum(
        own_row[0] * gate[0:1, :] + own_row[1] * gate[1:2, :], axis=1, keepdims=True
    )
    disp = own_row[0] + own_row[1]
    disp_b = disp.astype(BF)
    disp_t = disp.T.astype(BF)
    spread = jnp.where(lax.broadcasted_iota(jnp.int32, (FR, MK), 0) == pos[0:1, :], 1.0, 0.0)
    spread_b = spread.astype(BF)
    pick_b = spread.T.astype(BF)
    mrow_t = dot(disp_b, spread_b)

    def put_out(p, rows):
        for k in range(NS):
            out[p, k] = rows[2 * k : 2 * k + 2].astype(BF)

    def send_out(p):
        for k in range(1, NS):
            rc(out.at[p, k], inn.at[p, k], ds.at[p, k // 8], dr.at[p, k // 8], zpeer(k)).start()
        inn[p, 0] = out[p, 0]

    def span(ch):
        return pl.ds(8 * ch, 8) if ch else pl.ds(1, 7)

    def gather_in(p, ch):
        rc(out.at[p, span(ch)], inn.at[p, span(ch)], ds.at[p, ch], dr.at[p, ch], zup).wait_recv()
        rows = inn[p, 8 * ch : 8 * ch + 8].astype(F32).reshape(16, D).astype(BF)
        grp[p, ch, b, a] = rows
        blk = grp.at[p, ch, b, a]
        for d in (1, 2, 3):
            rc(blk, blk, gas.at[p, ch, d - 1], gar.at[p, ch, d - 1], apeer[d]).start()

    def gather_mid(p, ch):
        for d in (1, 2, 3):
            blk = grp.at[p, ch, b, (a + 4 - d) % 4]
            rc(blk, blk, gas.at[p, ch, d - 1], gar.at[p, ch, d - 1], apeer[d]).wait_recv()
        blk = grp.at[p, ch, b]
        for d in (1, 2, 3):
            rc(blk, blk, gbs.at[p, ch, d - 1], gbr.at[p, ch, d - 1], bpeer[d]).start()

    def work(p, ch):
        for d in (1, 2, 3):
            blk = grp.at[p, ch, (b + 4 - d) % 4]
            rc(blk, blk, gbs.at[p, ch, d - 1], gbr.at[p, ch, d - 1], bpeer[d]).wait_recv()
        rows = grp[p, ch].reshape(256, D)
        if p == 0:
            act, slp = gelu_parts(dot(rows, win[...]))
            act = act.astype(BF)
            part[p, ch] = dot(act, wout[...]).astype(BF).reshape(4, 4, 16, D)
        else:
            grad_pre = (dot(rows, woutt[...]) * slope[pl.ds(256 * ch, 256), :]).astype(BF)
            part[p, ch] = dot(grad_pre, wint[...]).astype(BF).reshape(4, 4, 16, D)
        for d in (1, 2, 3):
            rc(
                part.at[p, ch, (b + d) % 4], rsb.at[p, ch, d - 1], bs.at[p, ch, d - 1], br.at[p, ch, d - 1],
                bpeer[d],
            ).start()
        if p == 0:
            slope[pl.ds(256 * ch, 256), :] = slp
            act_t[:, 256 * ch : 256 * ch + 256] = act.T
            grp_t[:, 256 * ch : 256 * ch + 256] = rows.T
        else:
            gpre[pl.ds(256 * ch, 256), :] = grad_pre

    def reduce_b(p, ch):
        for d in (1, 2, 3):
            rc(
                part.at[p, ch, (b + d) % 4], rsb.at[p, ch, d - 1], bs.at[p, ch, d - 1], br.at[p, ch, d - 1],
                bpeer[d],
            ).wait_recv()
        total = (part[p, ch, b].astype(F32) + rsb[p, ch, 0].astype(F32)) + (
            rsb[p, ch, 1].astype(F32) + rsb[p, ch, 2].astype(F32)
        )
        acc[p, ch] = total.astype(BF)
        for d in (1, 2, 3):
            rc(
                acc.at[p, ch, (a + d) % 4], rsa.at[p, ch, d - 1], as_.at[p, ch, d - 1], ar.at[p, ch, d - 1],
                apeer[d],
            ).start()

    def reduce_a(p, ch):
        for d in (1, 2, 3):
            rc(
                acc.at[p, ch, (a + d) % 4], rsa.at[p, ch, d - 1], as_.at[p, ch, d - 1], ar.at[p, ch, d - 1],
                apeer[d],
            ).wait_recv()
        total = (acc[p, ch, a].astype(F32) + rsa[p, ch, 0].astype(F32)) + (
            rsa[p, ch, 1].astype(F32) + rsa[p, ch, 2].astype(F32)
        )
        rout[p, 8 * ch : 8 * ch + 8] = total.reshape(8, 2, D).astype(BF)
        for k in range(8 * ch, 8 * ch + 8):
            if k:
                rc(rout.at[p, k], ret.at[p, k], ts.at[p, ch], tr.at[p, ch], zback(k)).start()
        if ch == 0:
            ret[p, 0] = rout[p, 0]

    def returned(p):
        for ch in range(CHUNKS):
            rc(rout.at[p, span(ch)], ret.at[p, span(ch)], ts.at[p, ch], tr.at[p, ch], zup).wait_recv()
        return ret[p].astype(F32).reshape(ROWS, D).astype(BF)

    def sends_done(p):
        for ch in range(CHUNKS):
            rc(out.at[p, span(ch)], inn.at[p, span(ch)], ds.at[p, ch], dr.at[p, ch], zup).wait_send()
            rc(rout.at[p, span(ch)], ret.at[p, span(ch)], ts.at[p, ch], tr.at[p, ch], zup).wait_send()
            for d in (1, 2, 3):
                blk = grp.at[p, ch, b, a]
                rc(blk, blk, gas.at[p, ch, d - 1], gar.at[p, ch, d - 1], apeer[d]).wait_send()
                blk = grp.at[p, ch, b]
                rc(blk, blk, gbs.at[p, ch, d - 1], gbr.at[p, ch, d - 1], bpeer[d]).wait_send()
                rc(
                    part.at[p, ch, (b + d) % 4], rsb.at[p, ch, d - 1], bs.at[p, ch, d - 1],
                    br.at[p, ch, d - 1], bpeer[d],
                ).wait_send()
                rc(
                    acc.at[p, ch, (a + d) % 4], rsa.at[p, ch, d - 1], as_.at[p, ch, d - 1],
                    ar.at[p, ch, d - 1], apeer[d],
                ).wait_send()

    def ring_at(u):
        step, half = u // 2, u % 2
        up_half = half if u < 14 else 0
        dn_half = half if u < 14 else 1
        return step, up_half, dn_half

    def ring_copy(u, way):
        step, up_half, dn_half = ring_at(u)
        if way == 0:
            blk = tgt.at[(z + NZ - step) % NZ, c, up_half]
            return rc(blk, blk, rgs.at[0, u], rgr.at[0, u], zup)
        blk = tgt.at[(z + step) % NZ, c, dn_half]
        return rc(blk, blk, rgs.at[1, u], rgr.at[1, u], zdn)

    def ring_got(u, way):
        step, up_half, dn_half = ring_at(u)
        if way == 0:
            return tgt.at[(z + NZ - 1 - step) % NZ, c, up_half]
        return tgt.at[(z + 1 + step) % NZ, c, dn_half]

    def ring_take(u):
        for way in (0, 1):
            blk = ring_got(u, way)
            rc(blk, blk, rgs.at[way, u], rgr.at[way, u], zup).wait_recv()
            n = 2 + 2 * u + way
            rc(blk, blk, sbs.at[n], sbr.at[n], sib).start()

    def ring_step(u):
        if u == 0:
            for h in (0, 1):
                tloads[h].wait()
                blk = tgt.at[z, c, h]
                rc(blk, blk, sbs.at[h], sbr.at[h], sib).start()
        if 2 <= u != 15:
            ring_take(u - 2)
        if u == 14:
            ring_take(13)
        if u < 15:
            ring_copy(u, 0).start()
            ring_copy(u, 1).start()

    ring_next = [0]

    def ring_some(n):
        for _ in range(n):
            if ring_next[0] < 17:
                ring_step(ring_next[0])
                ring_next[0] += 1

    def shared_done():
        for h in (0, 1):
            blk = tgt.at[z, 1 - c, h]
            rc(blk, blk, sbs.at[h], sbr.at[h], sib).wait_recv()
        for u in range(15):
            step, up_half, dn_half = ring_at(u)
            for way in (0, 1):
                pos_z = (z + NZ - 1 - step) % NZ if way == 0 else (z + 1 + step) % NZ
                blk = tgt.at[pos_z, 1 - c, up_half if way == 0 else dn_half]
                n = 2 + 2 * u + way
                rc(blk, blk, sbs.at[n], sbr.at[n], sib).wait_recv()

    def ring_sends_done():
        for u in range(15):
            for way in (0, 1):
                ring_copy(u, way).wait_send()
                blk = ring_got(u, way)
                n = 2 + 2 * u + way
                rc(blk, blk, sbs.at[n], sbr.at[n], sib).wait_send()
        for h in (0, 1):
            blk = tgt.at[z, c, h]
            rc(blk, blk, sbs.at[h], sbr.at[h], sib).wait_send()

    stages = (gather_in, gather_mid, work, reduce_b, reduce_a)

    def flow(p):
        for t in range(CHUNKS + len(stages) - 1):
            for i in reversed(range(len(stages))):
                if 0 <= t - i < CHUNKS:
                    stages[i](p, t - i)
                    if p == 0 and t >= 1:
                        ring_some(1)

    put_out(0, dot(disp_b, hid[...]))
    pl.semaphore_wait(barrier, NS - 1 + 6)
    send_out(0)
    for cp in loads[5:]:
        cp.wait()
    picked_hidden = dot(pick_b, hid[...])
    wint[...] = win[...].T
    woutt[...] = wout[...].T
    flow(0)
    ring_some(17)

    lane = lax.broadcasted_iota(jnp.int32, (MK, NS * MK), 1)
    sub = lax.broadcasted_iota(jnp.int32, (MK, NS * MK), 0)
    own = jnp.where(lane == sub + s * MK, 1.0, 0.0)
    dis_f = jnp.concatenate([dis[...].astype(F32), jnp.zeros((16 - NEG, MK), F32)], axis=0).T
    lane_f = lane.astype(F32)
    count = own
    for j in range(NEG):
        count = count + jnp.where(dis_f[:, j : j + 1] == lane_f, 1.0, 0.0)
    shared_done()
    norms = []
    for q in range(NZ):
        v = tgt[q].reshape(2 * MK, D).astype(F32)
        n2 = jnp.sum(v * v, axis=1, keepdims=True)
        norms.append(jnp.broadcast_to(n2, (2 * MK, 128)).T[0:1, :])
    t_inv = 1.0 / jnp.sqrt(jnp.concatenate(norms, axis=1) + EPS)

    eout = returned(0)
    coef = (mrow_t * gate_row).T
    c_hi, c_lo = pieces(coef)
    mixed = picked_hidden + (dot(c_hi, eout) + dot(c_lo, eout))
    ctx_b = mixed.astype(BF)
    ctx = ctx_b.astype(F32)
    c_inv = 1.0 / jnp.sqrt(jnp.sum(ctx * ctx, axis=1, keepdims=True) + EPS)
    everyone = tgt[...].reshape(NS * MK, D)
    logits = dot_nt(ctx_b, everyone) * (c_inv * (1.0 / SHARP)) * t_inv
    log_total = jnp.log(jnp.sum(count * jnp.exp(logits), axis=1, keepdims=True))
    loss = log_total - jnp.sum(own * logits, axis=1, keepdims=True)
    lossv[:, :MK] = jnp.broadcast_to(loss, (MK, 128)).T[0:1, :]
    share = count * jnp.exp(logits - log_total)
    coef = (share - own) * (SCALE / SHARP) * t_inv
    c_hi, c_lo = pieces(coef)
    grad_unit = dot(c_hi, everyone) + dot(c_lo, everyone)
    ctx_unit = ctx * c_inv
    along = jnp.sum(grad_unit * ctx_unit, axis=1, keepdims=True)
    grad_ctx = (grad_unit - along * ctx_unit) * c_inv
    g_hi, g_lo = pieces(grad_ctx)
    g_two = jnp.concatenate([g_hi, g_lo], axis=0)

    mrow_b = mrow_t.astype(BF)
    grad_rows = dot(jnp.concatenate([mrow_b, mrow_b], axis=1), g_two) * gate_row
    put_out(1, grad_rows)
    send_out(1)
    q_two = dot_nt(eout, g_two)
    q_row = jnp.sum(mrow_t * (q_two[:, :MK] + q_two[:, MK:]), axis=1, keepdims=True)
    for t in (0, 1):
        ggv[t : t + 1, :] = jnp.sum(own_row[t] * q_row, axis=0, keepdims=True)
    grad_mixed = dot(jnp.concatenate([spread_b, spread_b], axis=1), g_two)
    outs = [
        pltpu.make_async_copy(lossv.at[:, pl.ds(0, 128)], loss_ref, osem.at[0]),
        pltpu.make_async_copy(ggv, gg_ref, osem.at[1]),
        pltpu.make_async_copy(dwov, dwo_ref, osem.at[2]),
        pltpu.make_async_copy(dwiv, dwi_ref, osem.at[3]),
        pltpu.make_async_copy(ghv, gh_ref, osem.at[4]),
    ]
    outs[0].start()
    outs[1].start()
    flow(1)

    grads = grp[1].reshape(16 * ROWS, D)
    for n in range(5):
        dwov[:, 256 * n : 256 * n + 256] = dot(act_t[...], grads[:, 256 * n : 256 * n + 256]).astype(BF)
    outs[2].start()
    gp = gpre[...]
    for n in range(5):
        dwiv[256 * n : 256 * n + 256, :] = dot(grp_t[256 * n : 256 * n + 256, :], gp).astype(BF)
    outs[3].start()
    ghv[...] = (grad_mixed + dot(disp_t, returned(1))).astype(BF)
    outs[4].start()
    ring_sends_done()
    sends_done(0)
    sends_done(1)
    for cp in outs:
        cp.wait()


def local(
    hidden, gate_probs, expert_ids, slot_ids, mask_pos, distractors, targets, weight_in, weight_out
):
    dma = pltpu.SemaphoreType.DMA
    vm = pltpu.VMEM
    hbm = pl.BlockSpec(memory_space=pl.ANY)
    outs = pl.pallas_call(
        kernel,
        out_shape=(
            jax.ShapeDtypeStruct((1, 128), F32),
            jax.ShapeDtypeStruct((2, FR), F32),
            jax.ShapeDtypeStruct((FR, D), BF),
            jax.ShapeDtypeStruct((D, HID), BF),
            jax.ShapeDtypeStruct((HID, D), BF),
        ),
        in_specs=[hbm] * 9,
        out_specs=(hbm,) * 5,
        scratch_shapes=[
            vm((FR, D), BF),
            vm((2, FR), F32),
            vm((2, FR), jnp.int32),
            vm((2, FR), jnp.int32),
            vm((1, MK), jnp.int32),
            vm((NEG, MK), jnp.int32),
            vm((D, HID), BF),
            vm((HID, D), BF),
            vm((HID, D), BF),
            vm((D, HID), BF),
            vm((NZ, 2, 2, 32, D), BF),
            vm((2, NS, 2, D), BF),
            vm((2, NS, 2, D), BF),
            vm((2, CHUNKS, 4, 4, 16, D), BF),
            vm((2, CHUNKS, 4, 4, 16, D), BF),
            vm((2, CHUNKS, 3, 4, 16, D), BF),
            vm((2, CHUNKS, 4, 16, D), BF),
            vm((2, CHUNKS, 3, 16, D), BF),
            vm((2, NS, 2, D), BF),
            vm((2, NS, 2, D), BF),
            vm((HID, 16 * ROWS), BF),
            vm((D, 16 * ROWS), BF),
            vm((16 * ROWS, HID), F32),
            vm((16 * ROWS, HID), BF),
            vm((1, 128), F32),
            vm((2, FR), F32),
            vm((FR, D), BF),
            vm((D, HID), BF),
            vm((HID, D), BF),
            dma((10,)),
            dma((5,)),
            dma((2, CHUNKS)),
            dma((2, CHUNKS)),
            dma((2, CHUNKS, 3)),
            dma((2, CHUNKS, 3)),
            dma((2, CHUNKS, 3)),
            dma((2, CHUNKS, 3)),
            dma((2, CHUNKS, 3)),
            dma((2, CHUNKS, 3)),
            dma((2, CHUNKS, 3)),
            dma((2, CHUNKS, 3)),
            dma((2, CHUNKS)),
            dma((2, CHUNKS)),
            dma((2, 15)),
            dma((2, 15)),
            dma((32,)),
            dma((32,)),
        ],
        compiler_params=pltpu.CompilerParams(
            collective_id=0, has_side_effects=True, vmem_limit_bytes=56 * 2**20
        ),
        cost_estimate=pl.CostEstimate(
            flops=6_000_000_000, bytes_accessed=8_000_000, transcendentals=1_000_000
        ),
        name="experts",
    )(
        hidden[0], gate_probs[0], expert_ids[0], slot_ids[0], mask_pos, distractors[0], targets[0],
        weight_in[0], weight_out[0],
    )
    loss, gate_grad, grad_hidden, grad_in, grad_out = outs
    return (loss[:, :MK], gate_grad[None], grad_hidden[None], grad_in[None], grad_out[None])


def solution(mesh):
    return jax.shard_map(
        local,
        mesh=mesh,
        in_specs=(
            P("dp", "seq", None),
            P("dp", None, "seq"),
            P("dp", None, "seq"),
            P("dp", None, "seq"),
            P("dp", "seq"),
            P("dp", None, "seq"),
            P("dp", "seq", None),
            P("seq", None, "dp"),
            P("seq", "dp", None),
        ),
        out_specs=(
            P("dp", "seq"),
            P("dp", None, "seq"),
            P("dp", "seq", None),
            P("seq", None, "dp"),
            P("seq", "dp", None),
        ),
        check_vma=False,
    )
```

time: 387 us -> 182 us (0.47)
  waiting for transfers between devices: 201 us -> 0 us
  Pallas kernels: 0 us -> 173 us
  blocking collectives: 55.3 us -> 0 us
  starting transfers between devices: 39.4 us -> 0 us
  local copies, waits for them, and re-layouts: 48 us -> 8.62 us
  matrix products: 15.8 us -> 0 us
  between operations: 14.3 us -> 0.68 us
  other arithmetic: 11.9 us -> 0 us
    pallas_call x0 -> x1, Pallas kernels: none -> 173 us  [local(): pl.pallas_call(kernel, out_shape=(jax.ShapeDtypeStruct((1, 128), F32), ja...]
    all_gather x3 -> x0, waiting for transfers between devices: 102 us -> none  [the longest x2 102 us: dispatch_rows(): return lax.all_gather(owned, 'dp', axis=0, tiled=True)]
    all_to_all x4 -> x0, waiting for transfers between devices: 98.2 us -> none  [the longest x2 70.2 us: collect_rows(): lax.all_to_all(partial_rows.astype(jnp.bfloat16), 'dp', split_axis=0, con...]
    all_to_all x2 -> x0, blocking collectives: 55.3 us -> none  [dispatch_rows(): lax.all_to_all(outgoing, 'seq', split_axis=0, concat_axis=0, tiled=True)]
    all_to_all x4 -> x0, starting transfers between devices: 39.1 us -> none  [the longest x2 30.5 us: collect_rows(): lax.all_to_all(summed.astype(jnp.bfloat16), 'seq', split_axis=0, concat_a...]
    convert_element_type x4 -> x0, local copies, waits for them, and re-layouts: 16.2 us -> none  [collect_rows(): partial_rows.astype(jnp.bfloat16)]
    dot_general x6 -> x0, matrix products: 15.8 us -> none  [the longest x1 3.83 us: local(): jnp.einsum('aecd,ehd->aech', grad_rows, weight_out, preferred_element_typ...]
    gather x7 -> x0, local copies, waits for them, and re-layouts: 13.7 us -> none  [the longest x1 7.71 us: local(): fetched = jnp.take(everyone, distractors[0].reshape(-1), axis=0)]
  transfers between devices with their start and end apart: 7 -> 0, of which waited for: 6 -> 0; matrix products, arithmetic and copies ran while one was open for 7% -> 0% of each run, Pallas kernels for 0% -> 0%
where the time goes in v1:
time: 182 us
  Pallas kernels  173 us (95%)
  local copies, waits for them, and re-layouts  8.62 us (5%)
    pallas_call x1, Pallas kernels, local(): pl.pallas_call(kernel, out_shape=(jax.ShapeDtypeStruct((1, 128), F32), ja...  173 us
    unnamed x17, local copies, waits for them, and re-layouts  8.62 us

profile of v1, /device:TPU:1, one launch (start us, length us, event | category | flops | bytes accessed | tf_op | source)
XLA Modules:
  0.0 181.8 jit_solution(3993814775873622171)
XLA Ops:
  0.6 0.0 copy-start.2
  0.6 0.7 copy-done.2
  1.3 0.6 copy.18
  1.9 2.2 %copy.14 = bf16[1,1280,320]{2,1,0:T(8,128)(2,1)} copy(bf16[1,1280,320]{1,2,0:T(8,128)(2,1)} %param.16) | data formatting | bytes 1638400 | tf_op args[7]
  4.1 172.5 %experts.1 = (f32[1,128]{1,0:T(1,128)}, f32[2,128]{1,0:T(2,128)}, bf16[128,1280]{1,0:T(8,128)(2,1)}, bf16[1280,320]{1,0:T(8,128)(2,1)}, bf16[320,1280]{1,0:T(8,128)(2,1)}) custom-call(bf16[128,1280]{1,0:T(8,128)(2,1)} %bitcast.22, f32[2,128]{1,0:T(2,128)} %bitcast.24, s32[2,128]{1,0:T(2,128)} %bitcast.25, s32[2,128]{1,0:T(2,128)} %bitcast.26, ...), custom_call_target="tpu_custom_call" | custom-call | flops 6000000000 | bytes 8000000 | tf_op jit(solution)/shard_map/experts/pallas_call | solution.py:408
  176.6 0.0 copy-start.4
  176.7 0.0 copy-start.1
  176.7 0.0 copy-start
  176.7 2.3 %copy.15 = bf16[1,1280,320]{1,2,0:T(8,128)(2,1)} copy(bf16[1,1280,320]{2,1,0:T(8,128)(2,1)} %bitcast.15) | data formatting | bytes 1638400
  178.9 0.0 copy-done.4
  178.9 0.0 copy-start.3
  179.0 0.5 copy.23
  179.5 0.2 copy-done.3
  179.6 0.6 copy.24
  180.2 0.0 copy-done.1
  180.2 0.7 copy.25
  180.9 0.0 copy-done
  180.9 0.9 copy.26
Async XLA Ops:
  0.6 0.7 copy-start.2
  176.6 2.3 %copy-start.4 = (f32[1,128]{1,0:T(1,128)S(1)}, f32[1,128]{1,0:T(1,128)}, u32[]{:S(2)}) copy-start(f32[1,128]{1,0:T(1,128)} %get-tuple-element.10) | copy-start | bytes 1540
  176.7 3.5 %copy-start.1 = (bf16[128,1280]{1,0:T(8,128)(2,1)S(1)}, bf16[128,1280]{1,0:T(8,128)(2,1)}, u32[]{:S(2)}) copy-start(bf16[128,1280]{1,0:T(8,128)(2,1)} %get-tuple-element.12) | copy-start | bytes 983044
  176.7 4.3 %copy-start = (bf16[320,1280]{1,0:T(8,128)(2,1)S(1)}, bf16[320,1280]{1,0:T(8,128)(2,1)}, u32[]{:S(2)}) copy-start(bf16[320,1280]{1,0:T(8,128)(2,1)} %get-tuple-element.14) | copy-start | bytes 2457604
  178.9 0.7 copy-start.3

commit v2 on v1

--- a/solution.py
+++ b/solution.py
@@ -20,6 +20,11 @@
 EPS = 1e-06
 SHARP = 0.1
 SCALE = 64.0
+ORDER = [
+    (0, 0), (0, 1), (1, 0), (0, 2), (1, 1), (2, 0), (0, 3), (1, 2), (2, 1), (1, 3), (2, 2), (3, 0),
+    (2, 3), (3, 1), (3, 2), (3, 3), (4, 0), (4, 1), (4, 2), (4, 3), (5, 0), (5, 1), (5, 2), (5, 3),
+    (6, 0), (6, 1), (6, 2), (6, 3),
+]
 DZ = [0] + [(h + 1) // 2 if h % 2 else NZ - h // 2 for h in range(1, NZ)]
 
 
@@ -51,7 +56,7 @@
     loss_ref, gg_ref, gh_ref, dwi_ref, dwo_ref,
     hid, gate, exps, slots, pos, dis, win, wout, wint, woutt,
     tgt, out, inn, grp, part, rsb, acc, rsa, rout, ret,
-    act_t, grp_t, slope, gpre, lossv, ggv, ghv, dwiv, dwov,
+    act_t, slope, gpre_t, lossv, ggv, ghv, dwiv, dwov,
     lsem, osem,
     ds, dr, gas, gar, gbs, gbr, bs, br, as_, ar, ts, tr,
     rgs, rgr, sbs, sbr,
@@ -83,16 +88,9 @@
             src_ref=src, dst_ref=dst, send_sem=ssem, recv_sem=rsem, device_id=dev, device_id_type=MESH
         )
 
-    barrier = pltpu.get_barrier_semaphore()
-    for k in range(1, NS):
-        pl.semaphore_signal(barrier, inc=1, device_id=zpeer(k), device_id_type=MESH)
-    for d in (1, 2, 3):
-        pl.semaphore_signal(barrier, inc=1, device_id=apeer[d], device_id_type=MESH)
-        pl.semaphore_signal(barrier, inc=1, device_id=bpeer[d], device_id_type=MESH)
-
     loads = [
         (hid_ref, hid), (gate_ref, gate), (exp_ref, exps), (slot_ref, slots), (pos_ref, pos),
-        (dis_ref, dis), (win_ref, win), (wout_ref, wout),
+        (dis_ref, dis), (win_ref, wint), (wout_ref, wout),
     ]
     loads = [pltpu.make_async_copy(p, q, lsem.at[i]) for i, (p, q) in enumerate(loads)]
     tloads = [
@@ -101,6 +99,13 @@
     ]
     for cp in loads + tloads:
         cp.start()
+    barrier = pltpu.get_barrier_semaphore()
+    for k in range(1, NS):
+        pl.semaphore_signal(barrier, inc=1, device_id=zpeer(k), device_id_type=MESH)
+    for d in (1, 2, 3):
+        pl.semaphore_signal(barrier, inc=1, device_id=apeer[d], device_id_type=MESH)
+        pl.semaphore_signal(barrier, inc=1, device_id=bpeer[d], device_id_type=MESH)
+
     for cp in loads[:5]:
         cp.wait()
 
@@ -148,14 +153,36 @@
         for d in (1, 2, 3):
             blk = grp.at[p, ch, b, (a + 4 - d) % 4]
             rc(blk, blk, gas.at[p, ch, d - 1], gar.at[p, ch, d - 1], apeer[d]).wait_recv()
-        blk = grp.at[p, ch, b]
-        for d in (1, 2, 3):
-            rc(blk, blk, gbs.at[p, ch, d - 1], gbr.at[p, ch, d - 1], bpeer[d]).start()
+        for slot in (0, 1):
+            b_copy(p, ch, slot).start()
+
+    def fore(ch):
+        return 1 if ch % 2 == 0 else 3
+
+    def b_copy(p, ch, slot):
+        g = fore(ch)
+        blk = grp.at[p, ch, (b + 4 - g) % 4] if slot == 2 else grp.at[p, ch, b]
+        dev = bpeer[4 - g] if slot == 1 else bpeer[g]
+        return rc(blk, blk, gbs.at[p, ch, slot], gbr.at[p, ch, slot], dev)
+
+    def b_wait(p, ch, slot):
+        g = fore(ch)
+        blk = grp.at[p, ch, (b + (4 - g, g, 2)[slot]) % 4]
+        rc(blk, blk, gbs.at[p, ch, slot], gbr.at[p, ch, slot], bpeer[g]).wait_recv()
+
+    def gather_on(p, ch):
+        b_wait(p, ch, 0)
+        b_copy(p, ch, 2).start()
+
+    def sum_copy(p, ch, slot):
+        g = fore(ch)
+        blk = part.at[p, ch, (b + (2, 4 - g, g)[slot]) % 4]
+        dev = bpeer[4 - g] if slot == 1 else bpeer[g]
+        return rc(blk, rsb.at[p, ch, slot], bs.at[p, ch, slot], br.at[p, ch, slot], dev)
 
     def work(p, ch):
-        for d in (1, 2, 3):
-            blk = grp.at[p, ch, (b + 4 - d) % 4]
-            rc(blk, blk, gbs.at[p, ch, d - 1], gbr.at[p, ch, d - 1], bpeer[d]).wait_recv()
+        b_wait(p, ch, 1)
+        b_wait(p, ch, 2)
         rows = grp[p, ch].reshape(256, D)
         if p == 0:
             act, slp = gelu_parts(dot(rows, win[...]))
@@ -164,27 +191,24 @@
         else:
             grad_pre = (dot(rows, woutt[...]) * slope[pl.ds(256 * ch, 256), :]).astype(BF)
             part[p, ch] = dot(grad_pre, wint[...]).astype(BF).reshape(4, 4, 16, D)
-        for d in (1, 2, 3):
-            rc(
-                part.at[p, ch, (b + d) % 4], rsb.at[p, ch, d - 1], bs.at[p, ch, d - 1], br.at[p, ch, d - 1],
-                bpeer[d],
-            ).start()
+        sum_copy(p, ch, 0).start()
+        sum_copy(p, ch, 1).start()
         if p == 0:
             slope[pl.ds(256 * ch, 256), :] = slp
             act_t[:, 256 * ch : 256 * ch + 256] = act.T
-            grp_t[:, 256 * ch : 256 * ch + 256] = rows.T
         else:
-            gpre[pl.ds(256 * ch, 256), :] = grad_pre
+            gpre_t[:, 256 * ch : 256 * ch + 256] = grad_pre.T
+
+    def reduce_on(p, ch):
+        nxt = (b + fore(ch)) % 4
+        sum_copy(p, ch, 0).wait_recv()
+        part[p, ch, nxt] = (part[p, ch, nxt].astype(F32) + rsb[p, ch, 0].astype(F32)).astype(BF)
+        sum_copy(p, ch, 2).start()
 
     def reduce_b(p, ch):
-        for d in (1, 2, 3):
-            rc(
-                part.at[p, ch, (b + d) % 4], rsb.at[p, ch, d - 1], bs.at[p, ch, d - 1], br.at[p, ch, d - 1],
-                bpeer[d],
-            ).wait_recv()
-        total = (part[p, ch, b].astype(F32) + rsb[p, ch, 0].astype(F32)) + (
-            rsb[p, ch, 1].astype(F32) + rsb[p, ch, 2].astype(F32)
-        )
+        sum_copy(p, ch, 1).wait_recv()
+        sum_copy(p, ch, 2).wait_recv()
+        total = part[p, ch, b].astype(F32) + (rsb[p, ch, 1].astype(F32) + rsb[p, ch, 2].astype(F32))
         acc[p, ch] = total.astype(BF)
         for d in (1, 2, 3):
             rc(
@@ -220,12 +244,8 @@
             for d in (1, 2, 3):
                 blk = grp.at[p, ch, b, a]
                 rc(blk, blk, gas.at[p, ch, d - 1], gar.at[p, ch, d - 1], apeer[d]).wait_send()
-                blk = grp.at[p, ch, b]
-                rc(blk, blk, gbs.at[p, ch, d - 1], gbr.at[p, ch, d - 1], bpeer[d]).wait_send()
-                rc(
-                    part.at[p, ch, (b + d) % 4], rsb.at[p, ch, d - 1], bs.at[p, ch, d - 1],
-                    br.at[p, ch, d - 1], bpeer[d],
-                ).wait_send()
+                b_copy(p, ch, d - 1).wait_send()
+                sum_copy(p, ch, d - 1).wait_send()
                 rc(
                     acc.at[p, ch, (a + d) % 4], rsa.at[p, ch, d - 1], as_.at[p, ch, d - 1],
                     ar.at[p, ch, d - 1], apeer[d],
@@ -303,15 +323,13 @@
             blk = tgt.at[z, c, h]
             rc(blk, blk, sbs.at[h], sbr.at[h], sib).wait_send()
 
-    stages = (gather_in, gather_mid, work, reduce_b, reduce_a)
+    stages = (gather_in, gather_mid, gather_on, work, reduce_on, reduce_b, reduce_a)
 
     def flow(p):
-        for t in range(CHUNKS + len(stages) - 1):
-            for i in reversed(range(len(stages))):
-                if 0 <= t - i < CHUNKS:
-                    stages[i](p, t - i)
-                    if p == 0 and t >= 1:
-                        ring_some(1)
+        for n, (i, ch) in enumerate(ORDER):
+            stages[i](p, ch)
+            if p == 0 and n >= 9:
+                ring_some(1)
 
     put_out(0, dot(disp_b, hid[...]))
     pl.semaphore_wait(barrier, NS - 1 + 6)
@@ -319,7 +337,7 @@
     for cp in loads[5:]:
         cp.wait()
     picked_hidden = dot(pick_b, hid[...])
-    wint[...] = win[...].T
+    win[...] = wint[...].T
     woutt[...] = wout[...].T
     flow(0)
     ring_some(17)
@@ -327,7 +345,7 @@
     lane = lax.broadcasted_iota(jnp.int32, (MK, NS * MK), 1)
     sub = lax.broadcasted_iota(jnp.int32, (MK, NS * MK), 0)
     own = jnp.where(lane == sub + s * MK, 1.0, 0.0)
-    dis_f = jnp.concatenate([dis[...].astype(F32), jnp.zeros((16 - NEG, MK), F32)], axis=0).T
+    dis_f = jnp.concatenate([dis[j].astype(F32) for j in range(NEG)] + [jnp.zeros((16 - NEG, MK), F32)], axis=0).T
     lane_f = lane.astype(F32)
     count = own
     for j in range(NEG):
@@ -386,9 +404,9 @@
     for n in range(5):
         dwov[:, 256 * n : 256 * n + 256] = dot(act_t[...], grads[:, 256 * n : 256 * n + 256]).astype(BF)
     outs[2].start()
-    gp = gpre[...]
+    rows = grp[0].reshape(16 * ROWS, D)
     for n in range(5):
-        dwiv[256 * n : 256 * n + 256, :] = dot(grp_t[256 * n : 256 * n + 256, :], gp).astype(BF)
+        dwiv[:, 256 * n : 256 * n + 256] = dot(gpre_t[...], rows[:, 256 * n : 256 * n + 256]).astype(BF)
     outs[3].start()
     ghv[...] = (grad_mixed + dot(disp_t, returned(1))).astype(BF)
     outs[4].start()
@@ -411,7 +429,7 @@
             jax.ShapeDtypeStruct((1, 128), F32),
             jax.ShapeDtypeStruct((2, FR), F32),
             jax.ShapeDtypeStruct((FR, D), BF),
-            jax.ShapeDtypeStruct((D, HID), BF),
+            jax.ShapeDtypeStruct((HID, D), BF),
             jax.ShapeDtypeStruct((HID, D), BF),
         ),
         in_specs=[hbm] * 9,
@@ -422,7 +440,7 @@
             vm((2, FR), jnp.int32),
             vm((2, FR), jnp.int32),
             vm((1, MK), jnp.int32),
-            vm((NEG, MK), jnp.int32),
+            vm((NEG, 1, MK), jnp.int32),
             vm((D, HID), BF),
             vm((HID, D), BF),
             vm((HID, D), BF),
@@ -438,13 +456,12 @@
             vm((2, NS, 2, D), BF),
             vm((2, NS, 2, D), BF),
             vm((HID, 16 * ROWS), BF),
-            vm((D, 16 * ROWS), BF),
             vm((16 * ROWS, HID), F32),
-            vm((16 * ROWS, HID), BF),
+            vm((HID, 16 * ROWS), BF),
             vm((1, 128), F32),
             vm((2, FR), F32),
             vm((FR, D), BF),
-            vm((D, HID), BF),
+            vm((HID, D), BF),
             vm((HID, D), BF),
             dma((10,)),
             dma((5,)),
@@ -473,11 +490,11 @@
         ),
         name="experts",
     )(
-        hidden[0], gate_probs[0], expert_ids[0], slot_ids[0], mask_pos, distractors[0], targets[0],
-        weight_in[0], weight_out[0],
+        hidden[0], gate_probs[0], expert_ids[0], slot_ids[0], mask_pos, jnp.swapaxes(distractors, 0, 1),
+        targets[0], weight_in[0].T, weight_out[0],
     )
     loss, gate_grad, grad_hidden, grad_in, grad_out = outs
-    return (loss[:, :MK], gate_grad[None], grad_hidden[None], grad_in[None], grad_out[None])
+    return (loss[:, :MK], gate_grad[None], grad_hidden[None], grad_in.T[None], grad_out[None])
 
 
 def solution(mesh):

time: 182 us -> 155 us (0.85)
  Pallas kernels: 173 us -> 147 us
  local copies, waits for them, and re-layouts: 8.62 us -> 6.56 us
    pallas_call x1, Pallas kernels: 173 us -> 147 us  [local(): pl.pallas_call(kernel, out_shape=(jax.ShapeDtypeStruct((1, 128), F32), ja...]
    unnamed x17 -> x11, local copies, waits for them, and re-layouts: 8.62 us -> 6.56 us
where the time goes in v2:
time: 155 us
  Pallas kernels  147 us (95%)
  local copies, waits for them, and re-layouts  6.56 us (4%)
    pallas_call x1, Pallas kernels, local(): pl.pallas_call(kernel, out_shape=(jax.ShapeDtypeStruct((1, 128), F32), ja...  147 us
    unnamed x11, local copies, waits for them, and re-layouts  6.56 us

profile of v2, /device:TPU:1, one launch (start us, length us, event | category | flops | bytes accessed | tf_op | source)
XLA Modules:
  0.0 154.6 jit_solution(1817605419578132550)
XLA Ops:
  0.6 147.4 %experts.1 = (f32[1,128]{1,0:T(1,128)}, f32[2,128]{1,0:T(2,128)}, bf16[128,1280]{1,0:T(8,128)(2,1)}, bf16[320,1280]{1,0:T(8,128)(2,1)}, bf16[320,1280]{1,0:T(8,128)(2,1)}) custom-call(bf16[128,1280]{1,0:T(8,128)(2,1)} %bitcast.23, f32[2,128]{1,0:T(2,128)} %bitcast.26, s32[2,128]{1,0:T(2,128)} %bitcast.27, s32[2,128]{1,0:T(2,128)} %bitcast.28, ...), custom_call_target="tpu_custom_call" | custom-call | flops 6000000000 | bytes 8000000 | tf_op jit(solution)/shard_map/experts/pallas_call | solution.py:426
  148.0 0.0 copy-start.2
  148.0 0.6 copy-done.2
  148.6 0.0 copy-start.1
  148.6 0.5 copy.19
  149.1 0.1 copy-done.1
  149.2 0.6 copy.20
  149.8 1.7 %copy.21 = bf16[1,128,1280]{2,1,0:T(8,128)(2,1)} copy(bf16[1,128,1280]{2,1,0:T(8,128)(2,1)} %bitcast.19) | data formatting | bytes 655360
  151.5 0.0 copy-start
  151.5 2.2 %copy.22 = bf16[1,1280,320]{1,2,0:T(8,128)(2,1)} copy(bf16[1,1280,320]{1,2,0:T(8,128)(2,1)} %bitcast.18) | data formatting | bytes 1638400
  153.7 0.0 copy-done
  153.7 0.9 copy.23
Async XLA Ops:
  148.0 0.6 copy-start.2
  148.6 0.7 copy-start.1
  151.5 2.2 %copy-start = (bf16[320,1280]{1,0:T(8,128)(2,1)S(1)}, bf16[320,1280]{1,0:T(8,128)(2,1)}, u32[]{:S(2)}) copy-start(bf16[320,1280]{1,0:T(8,128)(2,1)} %get-tuple-element.14) | copy-start | bytes 2457604

commit v3 on v2

--- a/solution.py
+++ b/solution.py
@@ -21,10 +21,11 @@
 SHARP = 0.1
 SCALE = 64.0
 ORDER = [
-    (0, 0), (0, 1), (1, 0), (0, 2), (1, 1), (2, 0), (0, 3), (1, 2), (2, 1), (1, 3), (2, 2), (3, 0),
+    (0, 0), (0, 1), (1, 0), (0, 2), (1, 1), (2, 0), (0, 3), (1, 2), (2, 1), (1, 3), (3, 0), (2, 2),
     (2, 3), (3, 1), (3, 2), (3, 3), (4, 0), (4, 1), (4, 2), (4, 3), (5, 0), (5, 1), (5, 2), (5, 3),
     (6, 0), (6, 1), (6, 2), (6, 3),
 ]
+FAR = (0, 3, 1, 2)
 DZ = [0] + [(h + 1) // 2 if h % 2 else NZ - h // 2 for h in range(1, NZ)]
 
 
@@ -118,16 +119,8 @@
     own_row = [
         jnp.where((exps[t : t + 1, :] == want) & (slots[t : t + 1, :] == cap), 1.0, 0.0) for t in (0, 1)
     ]
-    gate_row = jnp.sum(
-        own_row[0] * gate[0:1, :] + own_row[1] * gate[1:2, :], axis=1, keepdims=True
-    )
     disp = own_row[0] + own_row[1]
     disp_b = disp.astype(BF)
-    disp_t = disp.T.astype(BF)
-    spread = jnp.where(lax.broadcasted_iota(jnp.int32, (FR, MK), 0) == pos[0:1, :], 1.0, 0.0)
-    spread_b = spread.astype(BF)
-    pick_b = spread.T.astype(BF)
-    mrow_t = dot(disp_b, spread_b)
 
     def put_out(p, rows):
         for k in range(NS):
@@ -144,14 +137,14 @@
     def gather_in(p, ch):
         rc(out.at[p, span(ch)], inn.at[p, span(ch)], ds.at[p, ch], dr.at[p, ch], zup).wait_recv()
         rows = inn[p, 8 * ch : 8 * ch + 8].astype(F32).reshape(16, D).astype(BF)
-        grp[p, ch, b, a] = rows
-        blk = grp.at[p, ch, b, a]
+        grp[p, b, ch, a] = rows
+        blk = grp.at[p, b, ch, a]
         for d in (1, 2, 3):
             rc(blk, blk, gas.at[p, ch, d - 1], gar.at[p, ch, d - 1], apeer[d]).start()
 
     def gather_mid(p, ch):
         for d in (1, 2, 3):
-            blk = grp.at[p, ch, b, (a + 4 - d) % 4]
+            blk = grp.at[p, b, ch, (a + 4 - d) % 4]
             rc(blk, blk, gas.at[p, ch, d - 1], gar.at[p, ch, d - 1], apeer[d]).wait_recv()
         for slot in (0, 1):
             b_copy(p, ch, slot).start()
@@ -161,13 +154,13 @@
 
     def b_copy(p, ch, slot):
         g = fore(ch)
-        blk = grp.at[p, ch, (b + 4 - g) % 4] if slot == 2 else grp.at[p, ch, b]
+        blk = grp.at[p, (b + 4 - g) % 4, ch] if slot == 2 else grp.at[p, b, ch]
         dev = bpeer[4 - g] if slot == 1 else bpeer[g]
         return rc(blk, blk, gbs.at[p, ch, slot], gbr.at[p, ch, slot], dev)
 
     def b_wait(p, ch, slot):
         g = fore(ch)
-        blk = grp.at[p, ch, (b + (4 - g, g, 2)[slot]) % 4]
+        blk = grp.at[p, (b + (4 - g, g, 2)[slot]) % 4, ch]
         rc(blk, blk, gbs.at[p, ch, slot], gbr.at[p, ch, slot], bpeer[g]).wait_recv()
 
     def gather_on(p, ch):
@@ -176,39 +169,47 @@
 
     def sum_copy(p, ch, slot):
         g = fore(ch)
-        blk = part.at[p, ch, (b + (2, 4 - g, g)[slot]) % 4]
+        blk = part.at[p, (b + (2, 4 - g, g)[slot]) % 4, ch]
         dev = bpeer[4 - g] if slot == 1 else bpeer[g]
         return rc(blk, rsb.at[p, ch, slot], bs.at[p, ch, slot], br.at[p, ch, slot], dev)
 
-    def work(p, ch):
-        b_wait(p, ch, 1)
-        b_wait(p, ch, 2)
-        rows = grp[p, ch].reshape(256, D)
+    def work(p, u):
+        d = FAR[u]
+        at = (b + d) % 4
+        for ch in range(CHUNKS):
+            if d == 2:
+                b_wait(p, ch, 2)
+            elif d == fore(ch):
+                b_wait(p, ch, 1)
+        rows = grp[p, at].reshape(256, D)
         if p == 0:
             act, slp = gelu_parts(dot(rows, win[...]))
             act = act.astype(BF)
-            part[p, ch] = dot(act, wout[...]).astype(BF).reshape(4, 4, 16, D)
+            part[p, at] = dot(act, wout[...]).astype(BF).reshape(CHUNKS, 4, 16, D)
         else:
-            grad_pre = (dot(rows, woutt[...]) * slope[pl.ds(256 * ch, 256), :]).astype(BF)
-            part[p, ch] = dot(grad_pre, wint[...]).astype(BF).reshape(4, 4, 16, D)
-        sum_copy(p, ch, 0).start()
-        sum_copy(p, ch, 1).start()
+            grad_pre = (dot(rows, woutt[...]) * slope[at]).astype(BF)
+            part[p, at] = dot(grad_pre, wint[...]).astype(BF).reshape(CHUNKS, 4, 16, D)
+        for ch in range(CHUNKS):
+            if d == 2:
+                sum_copy(p, ch, 0).start()
+            elif d == 4 - fore(ch):
+                sum_copy(p, ch, 1).start()
         if p == 0:
-            slope[pl.ds(256 * ch, 256), :] = slp
-            act_t[:, 256 * ch : 256 * ch + 256] = act.T
+            slope[at] = slp
+            act_t[at] = act.T
         else:
-            gpre_t[:, 256 * ch : 256 * ch + 256] = grad_pre.T
+            gpre_t[at] = grad_pre.T
 
     def reduce_on(p, ch):
         nxt = (b + fore(ch)) % 4
         sum_copy(p, ch, 0).wait_recv()
-        part[p, ch, nxt] = (part[p, ch, nxt].astype(F32) + rsb[p, ch, 0].astype(F32)).astype(BF)
+        part[p, nxt, ch] = (part[p, nxt, ch].astype(F32) + rsb[p, ch, 0].astype(F32)).astype(BF)
         sum_copy(p, ch, 2).start()
 
     def reduce_b(p, ch):
         sum_copy(p, ch, 1).wait_recv()
         sum_copy(p, ch, 2).wait_recv()
-        total = part[p, ch, b].astype(F32) + (rsb[p, ch, 1].astype(F32) + rsb[p, ch, 2].astype(F32))
+        total = part[p, b, ch].astype(F32) + (rsb[p, ch, 1].astype(F32) + rsb[p, ch, 2].astype(F32))
         acc[p, ch] = total.astype(BF)
         for d in (1, 2, 3):
             rc(
@@ -242,7 +243,7 @@
             rc(out.at[p, span(ch)], inn.at[p, span(ch)], ds.at[p, ch], dr.at[p, ch], zup).wait_send()
             rc(rout.at[p, span(ch)], ret.at[p, span(ch)], ts.at[p, ch], tr.at[p, ch], zup).wait_send()
             for d in (1, 2, 3):
-                blk = grp.at[p, ch, b, a]
+                blk = grp.at[p, b, ch, a]
                 rc(blk, blk, gas.at[p, ch, d - 1], gar.at[p, ch, d - 1], apeer[d]).wait_send()
                 b_copy(p, ch, d - 1).wait_send()
                 sum_copy(p, ch, d - 1).wait_send()
@@ -334,6 +335,14 @@
     put_out(0, dot(disp_b, hid[...]))
     pl.semaphore_wait(barrier, NS - 1 + 6)
     send_out(0)
+    gate_row = jnp.sum(
+        own_row[0] * gate[0:1, :] + own_row[1] * gate[1:2, :], axis=1, keepdims=True
+    )
+    disp_t = disp.T.astype(BF)
+    spread = jnp.where(lax.broadcasted_iota(jnp.int32, (FR, MK), 0) == pos[0:1, :], 1.0, 0.0)
+    spread_b = spread.astype(BF)
+    pick_b = spread.T.astype(BF)
+    mrow_t = dot(disp_b, spread_b)
     for cp in loads[5:]:
         cp.wait()
     picked_hidden = dot(pick_b, hid[...])
@@ -400,13 +409,19 @@
     outs[1].start()
     flow(1)
 
-    grads = grp[1].reshape(16 * ROWS, D)
+    def over_rows(left, right, n):
+        total = dot(left[0], right[0, :, 256 * n : 256 * n + 256])
+        for g in range(1, 4):
+            total = total + dot(left[g], right[g, :, 256 * n : 256 * n + 256])
+        return total.astype(BF)
+
+    rows = grp[1].reshape(4, 4 * ROWS, D)
     for n in range(5):
-        dwov[:, 256 * n : 256 * n + 256] = dot(act_t[...], grads[:, 256 * n : 256 * n + 256]).astype(BF)
+        dwov[:, 256 * n : 256 * n + 256] = over_rows(act_t, rows, n)
     outs[2].start()
-    rows = grp[0].reshape(16 * ROWS, D)
+    rows = grp[0].reshape(4, 4 * ROWS, D)
     for n in range(5):
-        dwiv[:, 256 * n : 256 * n + 256] = dot(gpre_t[...], rows[:, 256 * n : 256 * n + 256]).astype(BF)
+        dwiv[:, 256 * n : 256 * n + 256] = over_rows(gpre_t, rows, n)
     outs[3].start()
     ghv[...] = (grad_mixed + dot(disp_t, returned(1))).astype(BF)
     outs[4].start()
@@ -455,9 +470,9 @@
             vm((2, CHUNKS, 3, 16, D), BF),
             vm((2, NS, 2, D), BF),
             vm((2, NS, 2, D), BF),
-            vm((HID, 16 * ROWS), BF),
-            vm((16 * ROWS, HID), F32),
-            vm((HID, 16 * ROWS), BF),
+            vm((4, HID, 4 * ROWS), BF),
+            vm((4, 4 * ROWS, HID), F32),
+            vm((4, HID, 4 * ROWS), BF),
             vm((1, 128), F32),
             vm((2, FR), F32),
             vm((FR, D), BF),

time: 155 us -> 159 us (1.026)
  Pallas kernels: 147 us -> 152 us
    pallas_call x1, Pallas kernels: 147 us -> 152 us  [local(): pl.pallas_call(kernel, out_shape=(jax.ShapeDtypeStruct((1, 128), F32), ja...]
where the time goes in v3:
time: 159 us
  Pallas kernels  152 us (96%)
  local copies, waits for them, and re-layouts  6.56 us (4%)
    pallas_call x1, Pallas kernels, local(): pl.pallas_call(kernel, out_shape=(jax.ShapeDtypeStruct((1, 128), F32), ja...  152 us
    unnamed x11, local copies, waits for them, and re-layouts  6.56 us

profile of v3, /device:TPU:1, one launch (start us, length us, event | category | flops | bytes accessed | tf_op | source)
XLA Modules:
  0.0 158.8 jit_solution(5755731722631543563)
XLA Ops:
  0.6 151.5 %experts.1 = (f32[1,128]{1,0:T(1,128)}, f32[2,128]{1,0:T(2,128)}, bf16[128,1280]{1,0:T(8,128)(2,1)}, bf16[320,1280]{1,0:T(8,128)(2,1)}, bf16[320,1280]{1,0:T(8,128)(2,1)}) custom-call(bf16[128,1280]{1,0:T(8,128)(2,1)} %bitcast.23, f32[2,128]{1,0:T(2,128)} %bitcast.26, s32[2,128]{1,0:T(2,128)} %bitcast.27, s32[2,128]{1,0:T(2,128)} %bitcast.28, ...), custom_call_target="tpu_custom_call" | custom-call | flops 6000000000 | bytes 8000000 | tf_op jit(solution)/shard_map/experts/pallas_call | solution.py:441
  152.2 0.0 copy-start.2
  152.2 0.6 copy-done.2
  152.8 0.0 copy-start.1
  152.8 0.5 copy.19
  153.3 0.1 copy-done.1
  153.4 0.6 copy.20
  154.0 1.7 %copy.21 = bf16[1,128,1280]{2,1,0:T(8,128)(2,1)} copy(bf16[1,128,1280]{2,1,0:T(8,128)(2,1)} %bitcast.19) | data formatting | bytes 655360
  155.7 0.0 copy-start
  155.7 2.2 %copy.22 = bf16[1,1280,320]{1,2,0:T(8,128)(2,1)} copy(bf16[1,1280,320]{1,2,0:T(8,128)(2,1)} %bitcast.18) | data formatting | bytes 1638400
  157.9 0.0 copy-done
  157.9 0.9 copy.23
Async XLA Ops:
  152.2 0.6 copy-start.2
  152.8 0.7 copy-start.1
  155.7 2.2 %copy-start = (bf16[320,1280]{1,0:T(8,128)(2,1)S(1)}, bf16[320,1280]{1,0:T(8,128)(2,1)}, u32[]{:S(2)}) copy-start(bf16[320,1280]{1,0:T(8,128)(2,1)} %get-tuple-element.14) | copy-start | bytes 2457604

commit v4 on v2

--- a/solution.py
+++ b/solution.py
@@ -25,6 +25,7 @@
     (2, 3), (3, 1), (3, 2), (3, 3), (4, 0), (4, 1), (4, 2), (4, 3), (5, 0), (5, 1), (5, 2), (5, 3),
     (6, 0), (6, 1), (6, 2), (6, 3),
 ]
+RING_AT = (4, 6, 8, 10, 11, 12, 13, 14, 15, 17, 19, 21, 23, 25, 27)
 DZ = [0] + [(h + 1) // 2 if h % 2 else NZ - h // 2 for h in range(1, NZ)]
 
 
@@ -56,7 +57,7 @@
     loss_ref, gg_ref, gh_ref, dwi_ref, dwo_ref,
     hid, gate, exps, slots, pos, dis, win, wout, wint, woutt,
     tgt, out, inn, grp, part, rsb, acc, rsa, rout, ret,
-    act_t, slope, gpre_t, lossv, ggv, ghv, dwiv, dwov,
+    act_t, slope, gpre_t, chosen, lossv, ggv, ghv, dwiv, dwov,
     lsem, osem,
     ds, dr, gas, gar, gbs, gbr, bs, br, as_, ar, ts, tr,
     rgs, rgr, sbs, sbr,
@@ -118,16 +119,8 @@
     own_row = [
         jnp.where((exps[t : t + 1, :] == want) & (slots[t : t + 1, :] == cap), 1.0, 0.0) for t in (0, 1)
     ]
-    gate_row = jnp.sum(
-        own_row[0] * gate[0:1, :] + own_row[1] * gate[1:2, :], axis=1, keepdims=True
-    )
     disp = own_row[0] + own_row[1]
     disp_b = disp.astype(BF)
-    disp_t = disp.T.astype(BF)
-    spread = jnp.where(lax.broadcasted_iota(jnp.int32, (FR, MK), 0) == pos[0:1, :], 1.0, 0.0)
-    spread_b = spread.astype(BF)
-    pick_b = spread.T.astype(BF)
-    mrow_t = dot(disp_b, spread_b)
 
     def put_out(p, rows):
         for k in range(NS):
@@ -328,12 +321,34 @@
     def flow(p):
         for n, (i, ch) in enumerate(ORDER):
             stages[i](p, ch)
-            if p == 0 and n >= 9:
+            if p == 0 and n in RING_AT:
                 ring_some(1)
+            if p == 0 and n == 19:
+                count_chosen()
+
+    lane = lax.broadcasted_iota(jnp.int32, (MK, NS * MK), 1)
+    sub = lax.broadcasted_iota(jnp.int32, (MK, NS * MK), 0)
+
+    def count_chosen():
+        rows = [dis[j].astype(F32) for j in range(NEG)] + [jnp.zeros((16 - NEG, MK), F32)]
+        dis_f = jnp.concatenate(rows, axis=0).T
+        lane_f = lane.astype(F32)
+        times = jnp.where(dis_f[:, 0:1] == lane_f, 1.0, 0.0)
+        for j in range(1, NEG):
+            times = times + jnp.where(dis_f[:, j : j + 1] == lane_f, 1.0, 0.0)
+        chosen[...] = times
 
     put_out(0, dot(disp_b, hid[...]))
     pl.semaphore_wait(barrier, NS - 1 + 6)
     send_out(0)
+    gate_row = jnp.sum(
+        own_row[0] * gate[0:1, :] + own_row[1] * gate[1:2, :], axis=1, keepdims=True
+    )
+    disp_t = disp.T.astype(BF)
+    spread = jnp.where(lax.broadcasted_iota(jnp.int32, (FR, MK), 0) == pos[0:1, :], 1.0, 0.0)
+    spread_b = spread.astype(BF)
+    pick_b = spread.T.astype(BF)
+    mrow_t = dot(disp_b, spread_b)
     for cp in loads[5:]:
         cp.wait()
     picked_hidden = dot(pick_b, hid[...])
@@ -342,14 +357,8 @@
     flow(0)
     ring_some(17)
 
-    lane = lax.broadcasted_iota(jnp.int32, (MK, NS * MK), 1)
-    sub = lax.broadcasted_iota(jnp.int32, (MK, NS * MK), 0)
     own = jnp.where(lane == sub + s * MK, 1.0, 0.0)
-    dis_f = jnp.concatenate([dis[j].astype(F32) for j in range(NEG)] + [jnp.zeros((16 - NEG, MK), F32)], axis=0).T
-    lane_f = lane.astype(F32)
-    count = own
-    for j in range(NEG):
-        count = count + jnp.where(dis_f[:, j : j + 1] == lane_f, 1.0, 0.0)
+    count = chosen[...] + own
     shared_done()
     norms = []
     for q in range(NZ):
@@ -458,6 +467,7 @@
             vm((HID, 16 * ROWS), BF),
             vm((16 * ROWS, HID), F32),
             vm((HID, 16 * ROWS), BF),
+            vm((MK, NS * MK), F32),
             vm((1, 128), F32),
             vm((2, FR), F32),
             vm((FR, D), BF),

time: 155 us -> 147 us (0.948)
  Pallas kernels: 147 us -> 140 us
    pallas_call x1, Pallas kernels: 147 us -> 140 us  [local(): pl.pallas_call(kernel, out_shape=(jax.ShapeDtypeStruct((1, 128), F32), ja...]
where the time goes in v4:
time: 147 us
  Pallas kernels  140 us (95%)
  local copies, waits for them, and re-layouts  6.56 us (4%)
    pallas_call x1, Pallas kernels, local(): pl.pallas_call(kernel, out_shape=(jax.ShapeDtypeStruct((1, 128), F32), ja...  140 us
    unnamed x11, local copies, waits for them, and re-layouts  6.56 us

profile of v4, /device:TPU:1, one launch (start us, length us, event | category | flops | bytes accessed | tf_op | source)
XLA Modules:
  0.0 147.1 jit_solution(903621643229008926)
XLA Ops:
  0.6 139.9 %experts.1 = (f32[1,128]{1,0:T(1,128)}, f32[2,128]{1,0:T(2,128)}, bf16[128,1280]{1,0:T(8,128)(2,1)}, bf16[320,1280]{1,0:T(8,128)(2,1)}, bf16[320,1280]{1,0:T(8,128)(2,1)}) custom-call(bf16[128,1280]{1,0:T(8,128)(2,1)} %bitcast.23, f32[2,128]{1,0:T(2,128)} %bitcast.26, s32[2,128]{1,0:T(2,128)} %bitcast.27, s32[2,128]{1,0:T(2,128)} %bitcast.28, ...), custom_call_target="tpu_custom_call" | custom-call | flops 6000000000 | bytes 8000000 | tf_op jit(solution)/shard_map/experts/pallas_call | solution.py:435
  140.5 0.0 copy-start.2
  140.5 0.6 copy-done.2
  141.1 0.0 copy-start.1
  141.1 0.5 copy.19
  141.6 0.1 copy-done.1
  141.7 0.6 copy.20
  142.3 1.7 %copy.21 = bf16[1,128,1280]{2,1,0:T(8,128)(2,1)} copy(bf16[1,128,1280]{2,1,0:T(8,128)(2,1)} %bitcast.19) | data formatting | bytes 655360
  144.0 0.0 copy-start
  144.0 2.2 %copy.22 = bf16[1,1280,320]{1,2,0:T(8,128)(2,1)} copy(bf16[1,1280,320]{1,2,0:T(8,128)(2,1)} %bitcast.18) | data formatting | bytes 1638400
  146.2 0.0 copy-done
  146.2 0.9 copy.23
Async XLA Ops:
  140.5 0.6 copy-start.2
  141.1 0.7 copy-start.1
  144.0 2.2 %copy-start = (bf16[320,1280]{1,0:T(8,128)(2,1)S(1)}, bf16[320,1280]{1,0:T(8,128)(2,1)}, u32[]{:S(2)}) copy-start(bf16[320,1280]{1,0:T(8,128)(2,1)} %get-tuple-element.14) | copy-start | bytes 2457604

commit v5 on v4

--- a/solution.py
+++ b/solution.py
@@ -25,7 +25,7 @@
     (2, 3), (3, 1), (3, 2), (3, 3), (4, 0), (4, 1), (4, 2), (4, 3), (5, 0), (5, 1), (5, 2), (5, 3),
     (6, 0), (6, 1), (6, 2), (6, 3),
 ]
-RING_AT = (4, 6, 8, 10, 11, 12, 13, 14, 15, 17, 19, 21, 23, 25, 27)
+RING_AT = (2, 4, 6, 8, 9, 10, 11, 12, 13, 14, 15, 17, 19, 21, 23)
 DZ = [0] + [(h + 1) // 2 if h % 2 else NZ - h // 2 for h in range(1, NZ)]
 
 

time: 147 us -> 146 us (level)
  Pallas kernels: 140 us -> 138 us
    pallas_call x1, Pallas kernels: 140 us -> 138 us  [local(): pl.pallas_call(kernel, out_shape=(jax.ShapeDtypeStruct((1, 128), F32), ja...]
where the time goes in v5:
time: 146 us
  Pallas kernels  138 us (95%)
  local copies, waits for them, and re-layouts  6.56 us (4%)
    pallas_call x1, Pallas kernels, local(): pl.pallas_call(kernel, out_shape=(jax.ShapeDtypeStruct((1, 128), F32), ja...  138 us
    unnamed x11, local copies, waits for them, and re-layouts  6.56 us

profile of v5, /device:TPU:1, one launch (start us, length us, event | category | flops | bytes accessed | tf_op | source)
XLA Modules:
  0.0 145.5 jit_solution(5790667879686964441)
XLA Ops:
  0.6 138.3 %experts.1 = (f32[1,128]{1,0:T(1,128)}, f32[2,128]{1,0:T(2,128)}, bf16[128,1280]{1,0:T(8,128)(2,1)}, bf16[320,1280]{1,0:T(8,128)(2,1)}, bf16[320,1280]{1,0:T(8,128)(2,1)}) custom-call(bf16[128,1280]{1,0:T(8,128)(2,1)} %bitcast.23, f32[2,128]{1,0:T(2,128)} %bitcast.26, s32[2,128]{1,0:T(2,128)} %bitcast.27, s32[2,128]{1,0:T(2,128)} %bitcast.28, ...), custom_call_target="tpu_custom_call" | custom-call | flops 6000000000 | bytes 8000000 | tf_op jit(solution)/shard_map/experts/pallas_call | solution.py:435
  138.9 0.0 copy-start.2
  138.9 0.6 copy-done.2
  139.5 0.0 copy-start.1
  139.5 0.5 copy.19
  140.0 0.1 copy-done.1
  140.2 0.6 copy.20
  140.7 1.7 %copy.21 = bf16[1,128,1280]{2,1,0:T(8,128)(2,1)} copy(bf16[1,128,1280]{2,1,0:T(8,128)(2,1)} %bitcast.19) | data formatting | bytes 655360
  142.5 0.0 copy-start
  142.5 2.2 %copy.22 = bf16[1,1280,320]{1,2,0:T(8,128)(2,1)} copy(bf16[1,1280,320]{1,2,0:T(8,128)(2,1)} %bitcast.18) | data formatting | bytes 1638400
  144.6 0.0 copy-done
  144.6 0.9 copy.23
Async XLA Ops:
  138.9 0.6 copy-start.2
  139.5 0.7 copy-start.1
  142.5 2.2 %copy-start = (bf16[320,1280]{1,0:T(8,128)(2,1)S(1)}, bf16[320,1280]{1,0:T(8,128)(2,1)}, u32[]{:S(2)}) copy-start(bf16[320,1280]{1,0:T(8,128)(2,1)} %get-tuple-element.14) | copy-start | bytes 2457604
